TPU v7x, 256 devices: a whole 4x4x8 slice. The times are simulated.
256 devices in a mesh: dp: 4 (over z_lo, core), seq: 64 (over z_hi, y, x).
Axes of the slice: x: 4, y: 4, z: 8 (z_hi: 4, z_lo: 2; z = z_hi * 2 + z_lo), core: 2. Of those that a mesh axis runs over, the one named last changes fastest.
Arguments:
- glu_out: bfloat16 [4, 8192, 1536], P('dp', 'seq'), may hold values from -6 to 6
- lengths: int32 [4], replicated, may hold values from 1024 to 8192, as said below
- kernel: float32 [31, 1536], replicated, may hold values from -1 to 1
- gain: float32 [1536], replicated, may hold values from 0.25 to 1.75
- bias: float32 [1536], replicated, may hold values from -3 to 3
- weight: bfloat16 [1536, 1536], P(('dp', 'seq')), may hold values from -0.15625 to 0.15625
- master: float32 [1536, 1536], P(('dp', 'seq')), may hold values from -0.15625 to 0.15625
- moment_one: float32 [1536, 1536], P(('dp', 'seq')), may hold values from -120 to 120
- moment_two: float32 [1536, 1536], P(('dp', 'seq')), may hold values from 100 to 100000
- cotangent: bfloat16 [4, 8192, 1536], P('dp', 'seq'), may hold values from -6 to 6
Outputs:
- module_out: bfloat16 [4, 8192, 1536], P('dp', 'seq')
- input_grad: bfloat16 [4, 8192, 1536], P('dp', 'seq')
- kernel_grad: float32 [31, 1536], replicated
- gain_grad: float32 [1536], replicated
- bias_grad: float32 [1536], replicated
- new_master: float32 [1536, 1536], P(('dp', 'seq'))
- new_one: float32 [1536, 1536], P(('dp', 'seq'))
- new_two: float32 [1536, 1536], P(('dp', 'seq'))
Inputs may be any that keep to these rules, and one draw needn't show every extreme that they name: `lengths`: in every draw one stream has all 8192 frames valid; each other stream has between 1024 and 2730 valid frames.
All inputs are finite; a program needn't handle non-finite values.
Results may differ from a plain program's by a relative error of at most 0.0049.
Values may be sent and summed in bfloat16 or wider, within the bound.
No kernel may reach another device: no remote copies, remote signals or barrier semaphores. Data moves between devices by JAX's collectives and lax.ppermute only.
A program may use at most 64 MiB of HBM per device.

v0:
```python
import jax
import jax.numpy as jnp
from jax import lax
from jax.sharding import PartitionSpec as P

KERNEL = 31
HALF = 15
beta_one = 0.9
beta_two = 0.999
adam_rate = 0.001
adam_eps = 1e-08
norm_eps = 1e-05
first_fix = 0.9999734386011124
second_fix = 0.09520785288629043


def with_halo(block, sides, width):
    for axis, dim in sides:
        count = lax.axis_size(axis)
        forward = [(i, i + 1) for i in range(count - 1)]
        backward = [(target, source) for source, target in forward]
        low = lax.ppermute(
            lax.slice_in_dim(block, block.shape[dim] - width, None, axis=dim), axis, forward
        )
        high = lax.ppermute(lax.slice_in_dim(block, 0, width, axis=dim), axis, backward)
        block = jnp.concatenate([low, block, high], axis=dim)
    return block


def on_device(
    glu_out, lengths, kernel, gain, bias, weight, master, moment_one, moment_two, cotangent
):
    frames = glu_out.shape[1]
    stream = lax.axis_index("dp")
    shard = lax.axis_index("seq")
    positions = shard * frames + jnp.arange(frames, dtype=jnp.int32)
    valid = (positions < lengths[stream])[:, None]
    count = jnp.sum(lengths).astype(jnp.float32)
    masked = jnp.where(valid, glu_out[0], jnp.zeros((), glu_out.dtype))
    padded = with_halo(masked, (("seq", 0),), HALF).astype(jnp.float32)
    conv_out = jnp.zeros((frames, masked.shape[1]), jnp.float32)
    for tap in range(KERNEL):
        conv_out = conv_out + kernel[tap] * padded[tap : tap + frames]
    total = lax.psum(jnp.sum(jnp.where(valid, conv_out, 0.0), axis=0), ("dp", "seq"))
    channel_mean = total / count
    deviation = jnp.where(valid, conv_out - channel_mean, 0.0)
    spread = lax.psum(jnp.sum(deviation * deviation, axis=0), ("dp", "seq"))
    channel_var = spread / count
    inv_std = lax.rsqrt(channel_var + norm_eps)
    standard = (conv_out - channel_mean) * inv_std
    scaled = gain * standard + bias
    logistic = jax.nn.sigmoid(scaled)
    hidden = (scaled * logistic).astype(jnp.bfloat16)
    grad_out = jnp.where(valid, cotangent[0], jnp.zeros((), cotangent.dtype))
    columns = hidden
    product = jnp.dot(
        columns,
        lax.all_gather(weight, ("dp", "seq"), axis=0, tiled=True),
        preferred_element_type=jnp.float32,
    )
    hidden_grad = lax.dot_general(
        grad_out,
        lax.all_gather(weight, ("dp", "seq"), axis=0, tiled=True),
        (((1,), (1,)), ((), ())),
        preferred_element_type=jnp.float32,
    )
    module_out = jnp.where(valid, product, 0.0).astype(jnp.bfloat16)
    scaled_grad = hidden_grad * logistic * (1.0 + scaled * (1.0 - logistic))
    gain_grad, bias_grad = lax.psum(
        (jnp.sum(scaled_grad * standard, axis=0), jnp.sum(scaled_grad, axis=0)), ("dp", "seq")
    )
    conv_grad = jnp.where(
        valid,
        inv_std
        * (gain * scaled_grad - gain * bias_grad / count - standard * gain * gain_grad / count),
        0.0,
    )
    grad_pad = with_halo(conv_grad, (("seq", 0),), HALF)
    flipped = jnp.zeros((frames, conv_grad.shape[1]), jnp.float32)
    for tap in range(KERNEL):
        flipped = flipped + kernel[tap] * grad_pad[2 * HALF - tap : 2 * HALF - tap + frames]
    input_grad = jnp.where(valid, flipped, 0.0).astype(jnp.bfloat16)
    tap_rows = []
    for tap in range(KERNEL):
        tap_rows.append(jnp.sum(conv_grad * padded[tap : tap + frames], axis=0))
    kernel_grad = lax.psum(jnp.stack(tap_rows), ("dp", "seq"))
    columns = hidden
    weight_grad = lax.psum_scatter(
        lax.dot_general(
            columns, grad_out, (((0,), (0,)), ((), ())), preferred_element_type=jnp.float32
        ),
        ("dp", "seq"),
        scatter_dimension=0,
        tiled=True,
    )
    new_one = beta_one * moment_one + (1.0 - beta_one) * weight_grad
    new_two = beta_two * moment_two + (1.0 - beta_two) * weight_grad * weight_grad
    new_master = master - adam_rate * (new_one / first_fix) / (
        jnp.sqrt(new_two / second_fix) + adam_eps
    )
    return (
        module_out[None],
        input_grad[None],
        kernel_grad,
        gain_grad,
        bias_grad,
        new_master,
        new_one,
        new_two,
    )


def solution(mesh):
    return jax.shard_map(
        on_device,
        mesh=mesh,
        in_specs=(
            P("dp", "seq", None),
            P(),
            P(),
            P(),
            P(),
            P(("dp", "seq"), None),
            P(("dp", "seq"), None),
            P(("dp", "seq"), None),
            P(("dp", "seq"), None),
            P("dp", "seq", None),
        ),
        out_specs=(
            P("dp", "seq", None),
            P("dp", "seq", None),
            P(),
            P(),
            P(),
            P(("dp", "seq"), None),
            P(("dp", "seq"), None),
            P(("dp", "seq"), None),
        ),
        check_vma=False,
    )
```

profile of v0, /device:TPU:1, one launch (start us, length us, event | category | flops | bytes accessed | tf_op | source)
XLA Modules:
  0.0 2008.2 jit_solution(8663492157685845760)
XLA Ops:
  25.6 85.3 %psum.35 = f32[1536]{0:T(1024)S(1)} all-reduce(f32[1536]{0:T(1024)S(1)} %get-tuple-element.78), channel_id=1, replica_groups=mesh['dp'=4,'seq'=64] {'dp','seq'}, use_global_device_ids=true, to_apply=%region_1.2 | all-reduce | flops 1536 | bytes 12288 | tf_op jit(solution)/shard_map/psum | solution.py:44
  111.1 73.7 %psum.36 = f32[1536]{0:T(1024)S(1)} all-reduce(f32[1536]{0:T(1024)S(1)} %multiply_reduce_fusion.32), channel_id=1, replica_groups=mesh['dp'=4,'seq'=64] {'dp','seq'}, use_global_device_ids=true, to_apply=%region_4.5 | all-reduce | flops 1536 | bytes 12288 | tf_op jit(solution)/shard_map/psum | solution.py:47
  190.0 808.0 %fusion = f32[8,1536]{1,0:T(8,128)S(1)} fusion(f32[1536,1536]{1,0:T(8,128)} %fusion.95), kind=kCustom, calls=%all-reduce-scatter | all-reduce-scatter fusion | flops 3145729 | bytes 9486336
  998.0 48.1 %collective-permute-start.66 = (f32[8,1536]{1,0:T(8,128)S(1)}, f32[8,1536]{1,0:T(8,128)S(1)}, u32[]{:S(2)}, u32[]{:S(2)}) collective-permute-start(f32[8,1536]{1,0:T(8,128)S(1)} %fusion), channel_id=1, source_target_pairs={{0,63},{1,64},{2,65},{3,66},{4,67},{5,68},{6,69},{7,70},{8,71},{9,... | collective-permute-start | bytes 147464
  1132.1 15.0 collective-permute-start.34
  1147.1 13.1 collective-permute-start.33
  1160.3 13.1 collective-permute-start.32
  1173.4 13.1 collective-permute-start.31
  1186.6 13.1 collective-permute-start.30
  1199.7 13.1 collective-permute-start.29
  1212.9 13.1 collective-permute-start.28
  1226.0 13.1 collective-permute-start.27
  1239.2 13.1 collective-permute-start.26
  1252.3 13.1 collective-permute-start.25
  1265.5 13.1 collective-permute-start.24
  1278.6 13.1 collective-permute-start.23
  1475.9 13.1 collective-permute-start.8
  1489.0 13.1 collective-permute-start.7
  1502.2 13.1 collective-permute-start.6
  1515.3 13.1 collective-permute-start.5
  1528.5 13.3 collective-permute-start.4
  1554.2 97.0 %concatenate.41 = f32[518,1536]{1,0:T(8,128)} concatenate(f32[6,1536]{1,0:T(8,128)S(1)} %collective-permute-done.67, f32[8,1536]{1,0:T(8,128)S(1)} %collective-permute-done.66, f32[8,1536]{1,0:T(8,128)S(1)} %collective-permute-done.65, f32[8,1536]{1,0:T(8,128)S(1)} %collective-permute-done.64, f32[8,1536]{1,0:T(8,128)S(1)} %collective-permute-done.63, ...), dimensions={0} | concatenate | bytes 6365184
  1665.4 72.6 %all-reduce.2 = (f32[1536]{0:T(1024)}, f32[1536]{0:T(1024)S(1)}) all-reduce(f32[1536]{0:T(1024)S(1)} %get-tuple-element.40, f32[1536]{0:T(1024)S(1)} %get-tuple-element.39), channel_id=1, replica_groups=mesh['dp'=4,'seq'=64] {'dp','seq'}, use_global_device_ids=true, to_apply=%region_8.9 | all-reduce | flops 3072 | bytes 24576 | tf_op jit(solution)/shard_map/psum | solution.py:69
  1755.6 244.2 %all-reduce.5.cloned.1.call-done = f32[31,1536]{1,0:T(8,128)} async-done(((f32[31,1536]{1,0:T(8,128)}), f32[31,1536]{1,0:T(8,128)}) %all-reduce.5.cloned.1.call-update) | async-done | bytes 190480 | tf_op jit(solution)/shard_map/psum | solution.py:86
  (306 shorter events, 337.0 us)
Async XLA Ops:
  7.2 1645.7 %all-gather.3.cloned.1.call-start = ((), (), s32[]{:S(2)}) async-start(), calls=%async_computation.1 | async-start | bytes 6316032 | tf_op jit(solution)/shard_map/all_gather | solution.py:58
  7.9 1991.8 %all-reduce.5.cloned.1.call-start = ((), (), s32[]{:S(2)}) async-start(), calls=%async_computation | async-start | bytes 393216 | tf_op jit(solution)/shard_map/psum | solution.py:86
  1132.1 67.6 %collective-permute-start.34 = (f32[8,1536]{1,0:T(8,128)S(1)}, f32[8,1536]{1,0:T(8,128)S(1)}, u32[]{:S(2)}, u32[]{:S(2)}) collective-permute-start(f32[8,1536]{1,0:T(8,128)S(1)} %fusion), channel_id=1, source_target_pairs={{0,31},{1,32},{2,33},{3,34},{4,35},{5,36},{6,37},{7,38},{8,39},{9,... | collective-permute-start | bytes 147464
  1147.1 65.7 %collective-permute-start.33 = (f32[8,1536]{1,0:T(8,128)S(1)}, f32[8,1536]{1,0:T(8,128)S(1)}, u32[]{:S(2)}, u32[]{:S(2)}) collective-permute-start(f32[8,1536]{1,0:T(8,128)S(1)} %fusion), channel_id=1, source_target_pairs={{0,30},{1,31},{2,32},{3,33},{4,34},{5,35},{6,36},{7,37},{8,38},{9,... | collective-permute-start | bytes 147464
  1160.3 65.7 %collective-permute-start.32 = (f32[8,1536]{1,0:T(8,128)S(1)}, f32[8,1536]{1,0:T(8,128)S(1)}, u32[]{:S(2)}, u32[]{:S(2)}) collective-permute-start(f32[8,1536]{1,0:T(8,128)S(1)} %fusion), channel_id=1, source_target_pairs={{0,29},{1,30},{2,31},{3,32},{4,33},{5,34},{6,35},{7,36},{8,37},{9,... | collective-permute-start | bytes 147464
  1173.4 65.7 %collective-permute-start.31 = (f32[8,1536]{1,0:T(8,128)S(1)}, f32[8,1536]{1,0:T(8,128)S(1)}, u32[]{:S(2)}, u32[]{:S(2)}) collective-permute-start(f32[8,1536]{1,0:T(8,128)S(1)} %fusion), channel_id=1, source_target_pairs={{0,28},{1,29},{2,30},{3,31},{4,32},{5,33},{6,34},{7,35},{8,36},{9,... | collective-permute-start | bytes 147464
  1186.6 65.7 %collective-permute-start.30 = (f32[8,1536]{1,0:T(8,128)S(1)}, f32[8,1536]{1,0:T(8,128)S(1)}, u32[]{:S(2)}, u32[]{:S(2)}) collective-permute-start(f32[8,1536]{1,0:T(8,128)S(1)} %fusion), channel_id=1, source_target_pairs={{0,27},{1,28},{2,29},{3,30},{4,31},{5,32},{6,33},{7,34},{8,35},{9,... | collective-permute-start | bytes 147464
  1199.7 65.7 %collective-permute-start.29 = (f32[8,1536]{1,0:T(8,128)S(1)}, f32[8,1536]{1,0:T(8,128)S(1)}, u32[]{:S(2)}, u32[]{:S(2)}) collective-permute-start(f32[8,1536]{1,0:T(8,128)S(1)} %fusion), channel_id=1, source_target_pairs={{0,26},{1,27},{2,28},{3,29},{4,30},{5,31},{6,32},{7,33},{8,34},{9,... | collective-permute-start | bytes 147464
  1212.9 65.7 %collective-permute-start.28 = (f32[8,1536]{1,0:T(8,128)S(1)}, f32[8,1536]{1,0:T(8,128)S(1)}, u32[]{:S(2)}, u32[]{:S(2)}) collective-permute-start(f32[8,1536]{1,0:T(8,128)S(1)} %fusion), channel_id=1, source_target_pairs={{0,25},{1,26},{2,27},{3,28},{4,29},{5,30},{6,31},{7,32},{8,33},{9,... | collective-permute-start | bytes 147464
  1226.0 65.7 %collective-permute-start.27 = (f32[8,1536]{1,0:T(8,128)S(1)}, f32[8,1536]{1,0:T(8,128)S(1)}, u32[]{:S(2)}, u32[]{:S(2)}) collective-permute-start(f32[8,1536]{1,0:T(8,128)S(1)} %fusion), channel_id=1, source_target_pairs={{0,24},{1,25},{2,26},{3,27},{4,28},{5,29},{6,30},{7,31},{8,32},{9,... | collective-permute-start | bytes 147464
  1239.2 65.7 %collective-permute-start.26 = (f32[8,1536]{1,0:T(8,128)S(1)}, f32[8,1536]{1,0:T(8,128)S(1)}, u32[]{:S(2)}, u32[]{:S(2)}) collective-permute-start(f32[8,1536]{1,0:T(8,128)S(1)} %fusion), channel_id=1, source_target_pairs={{0,23},{1,24},{2,25},{3,26},{4,27},{5,28},{6,29},{7,30},{8,31},{9,... | collective-permute-start | bytes 147464
  1252.3 65.7 %collective-permute-start.25 = (f32[8,1536]{1,0:T(8,128)S(1)}, f32[8,1536]{1,0:T(8,128)S(1)}, u32[]{:S(2)}, u32[]{:S(2)}) collective-permute-start(f32[8,1536]{1,0:T(8,128)S(1)} %fusion), channel_id=1, source_target_pairs={{0,22},{1,23},{2,24},{3,25},{4,26},{5,27},{6,28},{7,29},{8,30},{9,... | collective-permute-start | bytes 147464
  1265.5 65.7 %collective-permute-start.24 = (f32[8,1536]{1,0:T(8,128)S(1)}, f32[8,1536]{1,0:T(8,128)S(1)}, u32[]{:S(2)}, u32[]{:S(2)}) collective-permute-start(f32[8,1536]{1,0:T(8,128)S(1)} %fusion), channel_id=1, source_target_pairs={{0,21},{1,22},{2,23},{3,24},{4,25},{5,26},{6,27},{7,28},{8,29},{9,... | collective-permute-start | bytes 147464
  1278.6 65.7 %collective-permute-start.23 = (f32[8,1536]{1,0:T(8,128)S(1)}, f32[8,1536]{1,0:T(8,128)S(1)}, u32[]{:S(2)}, u32[]{:S(2)}) collective-permute-start(f32[8,1536]{1,0:T(8,128)S(1)} %fusion), channel_id=1, source_target_pairs={{0,20},{1,21},{2,22},{3,23},{4,24},{5,25},{6,26},{7,27},{8,28},{9,... | collective-permute-start | bytes 147464
  1291.8 65.7 %collective-permute-start.22 = (f32[8,1536]{1,0:T(8,128)S(1)}, f32[8,1536]{1,0:T(8,128)S(1)}, u32[]{:S(2)}, u32[]{:S(2)}) collective-permute-start(f32[8,1536]{1,0:T(8,128)S(1)} %fusion), channel_id=1, source_target_pairs={{0,19},{1,20},{2,21},{3,22},{4,23},{5,24},{6,25},{7,26},{8,27},{9,... | collective-permute-start | bytes 147464
  1304.9 65.7 %collective-permute-start.21 = (f32[8,1536]{1,0:T(8,128)S(1)}, f32[8,1536]{1,0:T(8,128)S(1)}, u32[]{:S(2)}, u32[]{:S(2)}) collective-permute-start(f32[8,1536]{1,0:T(8,128)S(1)} %fusion), channel_id=1, source_target_pairs={{0,18},{1,19},{2,20},{3,21},{4,22},{5,23},{6,24},{7,25},{8,26},{9,... | collective-permute-start | bytes 147464
  1318.1 65.7 %collective-permute-start.20 = (f32[8,1536]{1,0:T(8,128)S(1)}, f32[8,1536]{1,0:T(8,128)S(1)}, u32[]{:S(2)}, u32[]{:S(2)}) collective-permute-start(f32[8,1536]{1,0:T(8,128)S(1)} %fusion), channel_id=1, source_target_pairs={{0,17},{1,18},{2,19},{3,20},{4,21},{5,22},{6,23},{7,24},{8,25},{9,... | collective-permute-start | bytes 147464
  1331.2 65.7 %collective-permute-start.19 = (f32[8,1536]{1,0:T(8,128)S(1)}, f32[8,1536]{1,0:T(8,128)S(1)}, u32[]{:S(2)}, u32[]{:S(2)}) collective-permute-start(f32[8,1536]{1,0:T(8,128)S(1)} %fusion), channel_id=1, source_target_pairs={{0,16},{1,17},{2,18},{3,19},{4,20},{5,21},{6,22},{7,23},{8,24},{9,... | collective-permute-start | bytes 147464
  1344.4 65.7 %collective-permute-start.18 = (f32[8,1536]{1,0:T(8,128)S(1)}, f32[8,1536]{1,0:T(8,128)S(1)}, u32[]{:S(2)}, u32[]{:S(2)}) collective-permute-start(f32[8,1536]{1,0:T(8,128)S(1)} %fusion), channel_id=1, source_target_pairs={{0,15},{1,16},{2,17},{3,18},{4,19},{5,20},{6,21},{7,22},{8,23},{9,... | collective-permute-start | bytes 147464
  1423.3 65.7 %collective-permute-start.12 = (f32[8,1536]{1,0:T(8,128)S(1)}, f32[8,1536]{1,0:T(8,128)S(1)}, u32[]{:S(2)}, u32[]{:S(2)}) collective-permute-start(f32[8,1536]{1,0:T(8,128)S(1)} %fusion), channel_id=1, source_target_pairs={{0,9},{1,10},{2,11},{3,12},{4,13},{5,14},{6,15},{7,16},{8,17},{9,1... | collective-permute-start | bytes 147464
  1436.4 65.7 %collective-permute-start.11 = (f32[8,1536]{1,0:T(8,128)S(1)}, f32[8,1536]{1,0:T(8,128)S(1)}, u32[]{:S(2)}, u32[]{:S(2)}) collective-permute-start(f32[8,1536]{1,0:T(8,128)S(1)} %fusion), channel_id=1, source_target_pairs={{0,8},{1,9},{2,10},{3,11},{4,12},{5,13},{6,14},{7,15},{8,16},{9,17... | collective-permute-start | bytes 147464
  1449.6 65.7 %collective-permute-start.10 = (f32[8,1536]{1,0:T(8,128)S(1)}, f32[8,1536]{1,0:T(8,128)S(1)}, u32[]{:S(2)}, u32[]{:S(2)}) collective-permute-start(f32[8,1536]{1,0:T(8,128)S(1)} %fusion), channel_id=1, source_target_pairs={{0,7},{1,8},{2,9},{3,10},{4,11},{5,12},{6,13},{7,14},{8,15},{9,16}... | collective-permute-start | bytes 147464
  1462.7 65.7 %collective-permute-start.9 = (f32[8,1536]{1,0:T(8,128)S(1)}, f32[8,1536]{1,0:T(8,128)S(1)}, u32[]{:S(2)}, u32[]{:S(2)}) collective-permute-start(f32[8,1536]{1,0:T(8,128)S(1)} %fusion), channel_id=1, source_target_pairs={{0,6},{1,7},{2,8},{3,9},{4,10},{5,11},{6,12},{7,13},{8,14},{9,15},... | collective-permute-start | bytes 147464
  1475.9 66.3 %collective-permute-start.8 = (f32[8,1536]{1,0:T(8,128)S(1)}, f32[8,1536]{1,0:T(8,128)}, u32[]{:S(2)}, u32[]{:S(2)}) collective-permute-start(f32[8,1536]{1,0:T(8,128)S(1)} %fusion), channel_id=1, source_target_pairs={{0,5},{1,6},{2,7},{3,8},{4,9},{5,10},{6,11},{7,12},{8,13},{9,14},{... | collective-permute-start | bytes 147464
  (109 other events, 10515.9 us)
Sparse Core Ops, SparseCore 0:
  9.9 738.2 all-gather.2
  1751.2 248.4 all-reduce.4
where the time goes:
time: 2010 us
  blocking collectives  1040 us (52%)
  starting transfers between devices  550 us (27%)
  waiting for transfers between devices  259 us (13%)
  local copies, waits for them, and re-layouts  115 us (6%)
    unnamed x1, blocking collectives  808 us
    unnamed x64, starting transfers between devices  541 us
    psum x1, waiting for transfers between devices, on_device(): kernel_grad = lax.psum(jnp.stack(tap_rows), ('dp', 'seq'))  244 us
    unnamed x130, local copies, waits for them, and re-layouts  108 us
    psum x1, blocking collectives, on_device(): lax.psum(jnp.sum(jnp.where(valid, conv_out, 0.0), axis=0), ('dp', 'seq'))  85.3 us
    psum x1, blocking collectives, on_device(): spread = lax.psum(jnp.sum(deviation * deviation, axis=0), ('dp', 'seq'))  73.7 us
    psum x1, blocking collectives, on_device(): lax.psum((jnp.sum(scaled_grad * standard, axis=0), jnp.sum(scaled_grad, a...  72.6 us
  transfers between devices with their start and end apart: 70, of which 3 were waited for; matrix products, arithmetic and copies ran while one was open for 46% of the time, Pallas kernels for 0%

commit v1 on v0

--- a/solution.py
+++ b/solution.py
@@ -66,8 +66,11 @@
     )
     module_out = jnp.where(valid, product, 0.0).astype(jnp.bfloat16)
     scaled_grad = hidden_grad * logistic * (1.0 + scaled * (1.0 - logistic))
-    gain_grad, bias_grad = lax.psum(
-        (jnp.sum(scaled_grad * standard, axis=0), jnp.sum(scaled_grad, axis=0)), ("dp", "seq")
+    _cut_pools = lambda inner_x: jax.lax.psum(
+        jax.lax.psum(inner_x, axis_name="dp"), axis_name="seq"
+    )
+    gain_grad, bias_grad = _cut_pools(
+        (jnp.sum(scaled_grad * standard, axis=0), jnp.sum(scaled_grad, axis=0))
     )
     conv_grad = jnp.where(
         valid,

time: 2010 us -> 2340 us (1.16)
  blocking collectives: 1040 us -> 1280 us
  waiting for transfers between devices: 259 us -> 314 us
  starting transfers between devices: 550 us -> 580 us
    psum x1 -> x2, blocking collectives: 72.6 us -> 324 us  [the longest x1 315 us: on_device(): jax.lax.psum(jax.lax.psum(inner_x, axis_name='dp'), axis_name='seq')]
    psum x1, waiting for transfers between devices: 244 us -> 300 us  [on_device(): kernel_grad = lax.psum(jnp.stack(tap_rows), ('dp', 'seq'))]
    unnamed x64, starting transfers between devices: 541 us -> 571 us
  transfers between devices with their start and end apart: 70 -> 70, of which waited for: 3 -> 3; matrix products, arithmetic and copies ran while one was open for 46% -> 39% of each run, Pallas kernels for 0% -> 0%
where the time goes in v1:
time: 2340 us
  blocking collectives  1280 us (55%)
  starting transfers between devices  580 us (25%)
  waiting for transfers between devices  314 us (13%)
  local copies, waits for them, and re-layouts  115 us (5%)
    unnamed x1, blocking collectives  799 us
    unnamed x64, starting transfers between devices  571 us
    psum x1, blocking collectives, on_device(): jax.lax.psum(jax.lax.psum(inner_x, axis_name='dp'), axis_name='seq')  315 us
    psum x1, waiting for transfers between devices, on_device(): kernel_grad = lax.psum(jnp.stack(tap_rows), ('dp', 'seq'))  300 us
    unnamed x130, local copies, waits for them, and re-layouts  108 us
    psum x1, blocking collectives, on_device(): lax.psum(jnp.sum(jnp.where(valid, conv_out, 0.0), axis=0), ('dp', 'seq'))  85.3 us
    psum x1, blocking collectives, on_device(): spread = lax.psum(jnp.sum(deviation * deviation, axis=0), ('dp', 'seq'))  73.7 us
  transfers between devices with their start and end apart: 70, of which 3 were waited for; matrix products, arithmetic and copies ran while one was open for 39% of the time, Pallas kernels for 0%

profile of v1, /device:TPU:1, one launch (start us, length us, event | category | flops | bytes accessed | tf_op | source)
XLA Modules:
  0.0 2336.2 jit_solution(9792577715766506649)
XLA Ops:
  25.6 85.3 %psum.49 = f32[1536]{0:T(1024)S(1)} all-reduce(f32[1536]{0:T(1024)S(1)} %get-tuple-element.80), channel_id=1, replica_groups=mesh['dp'=4,'seq'=64] {'dp','seq'}, use_global_device_ids=true, to_apply=%region_1.2 | all-reduce | flops 1536 | bytes 12288 | tf_op jit(solution)/shard_map/psum | solution.py:44
  111.1 73.7 %psum.50 = f32[1536]{0:T(1024)S(1)} all-reduce(f32[1536]{0:T(1024)S(1)} %multiply_reduce_fusion.32), channel_id=1, replica_groups=mesh['dp'=4,'seq'=64] {'dp','seq'}, use_global_device_ids=true, to_apply=%region_4.5 | all-reduce | flops 1536 | bytes 12288 | tf_op jit(solution)/shard_map/psum | solution.py:47
  190.0 798.7 %fusion = f32[8,1536]{1,0:T(8,128)S(1)} fusion(f32[1536,1536]{1,0:T(8,128)} %fusion.95), kind=kCustom, calls=%all-reduce-scatter | all-reduce-scatter fusion | flops 3145729 | bytes 9486336
  988.7 57.5 %collective-permute-start.66 = (f32[8,1536]{1,0:T(8,128)S(1)}, f32[8,1536]{1,0:T(8,128)S(1)}, u32[]{:S(2)}, u32[]{:S(2)}) collective-permute-start(f32[8,1536]{1,0:T(8,128)S(1)} %fusion), channel_id=1, source_target_pairs={{0,63},{1,64},{2,65},{3,66},{4,67},{5,68},{6,69},{7,70},{8,71},{9,... | collective-permute-start | bytes 147464
  1126.5 14.6 collective-permute-start.36
  1141.1 13.1 collective-permute-start.35
  1154.2 13.1 collective-permute-start.34
  1167.4 13.1 collective-permute-start.33
  1180.5 13.1 collective-permute-start.32
  1193.7 13.1 collective-permute-start.31
  1206.8 13.1 collective-permute-start.30
  1220.0 13.1 collective-permute-start.29
  1233.1 13.1 collective-permute-start.28
  1246.3 13.1 collective-permute-start.27
  1259.4 13.1 collective-permute-start.26
  1272.6 13.1 collective-permute-start.25
  1496.1 13.1 collective-permute-start.8
  1509.3 13.1 collective-permute-start.7
  1522.4 13.1 collective-permute-start.6
  1535.6 13.1 collective-permute-start.5
  1548.7 13.3 collective-permute-start.4
  1574.5 97.0 %concatenate.41 = f32[518,1536]{1,0:T(8,128)} concatenate(f32[6,1536]{1,0:T(8,128)S(1)} %collective-permute-done.67, f32[8,1536]{1,0:T(8,128)S(1)} %collective-permute-done.66, f32[8,1536]{1,0:T(8,128)S(1)} %collective-permute-done.65, f32[8,1536]{1,0:T(8,128)S(1)} %collective-permute-done.64, f32[8,1536]{1,0:T(8,128)S(1)} %collective-permute-done.63, ...), dimensions={0} | concatenate | bytes 6365184
  1695.1 315.0 %all-reduce.2 = (f32[1536]{0:T(1024)}, f32[1536]{0:T(1024)S(1)}) all-reduce(f32[1536]{0:T(1024)S(1)} %get-tuple-element.74, f32[1536]{0:T(1024)S(1)} %get-tuple-element.75), channel_id=1, replica_groups=mesh['dp'=4,'seq'=64] {'seq'}, use_global_device_ids=true, to_apply=%region_10.11 | all-reduce | flops 3072 | bytes 24576 | tf_op jit(solution)/shard_map/psum | solution.py:69
  2027.3 300.4 %all-reduce.6.cloned.1.call-done = f32[31,1536]{1,0:T(8,128)} async-done(((f32[31,1536]{1,0:T(8,128)}), f32[31,1536]{1,0:T(8,128)}) %all-reduce.6.cloned.1.call-update) | async-done | bytes 190480 | tf_op jit(solution)/shard_map/psum | solution.py:89
  (307 shorter events, 366.7 us)
Async XLA Ops:
  7.2 1665.9 %all-gather.3.cloned.1.call-start = ((), (), s32[]{:S(2)}) async-start(), calls=%async_computation.1 | async-start | bytes 6316032 | tf_op jit(solution)/shard_map/all_gather | solution.py:58
  7.9 2319.8 %all-reduce.6.cloned.1.call-start = ((), (), s32[]{:S(2)}) async-start(), calls=%async_computation | async-start | bytes 393216 | tf_op jit(solution)/shard_map/psum | solution.py:89
  988.7 69.2 %collective-permute-start.66 = (f32[8,1536]{1,0:T(8,128)S(1)}, f32[8,1536]{1,0:T(8,128)S(1)}, u32[]{:S(2)}, u32[]{:S(2)}) collective-permute-start(f32[8,1536]{1,0:T(8,128)S(1)} %fusion), channel_id=1, source_target_pairs={{0,63},{1,64},{2,65},{3,66},{4,67},{5,68},{6,69},{7,70},{8,71},{9,... | collective-permute-start | bytes 147464
  1126.5 67.2 %collective-permute-start.36 = (f32[8,1536]{1,0:T(8,128)S(1)}, f32[8,1536]{1,0:T(8,128)S(1)}, u32[]{:S(2)}, u32[]{:S(2)}) collective-permute-start(f32[8,1536]{1,0:T(8,128)S(1)} %fusion), channel_id=1, source_target_pairs={{0,33},{1,34},{2,35},{3,36},{4,37},{5,38},{6,39},{7,40},{8,41},{9,... | collective-permute-start | bytes 147464
  1141.1 65.7 %collective-permute-start.35 = (f32[8,1536]{1,0:T(8,128)S(1)}, f32[8,1536]{1,0:T(8,128)S(1)}, u32[]{:S(2)}, u32[]{:S(2)}) collective-permute-start(f32[8,1536]{1,0:T(8,128)S(1)} %fusion), channel_id=1, source_target_pairs={{0,32},{1,33},{2,34},{3,35},{4,36},{5,37},{6,38},{7,39},{8,40},{9,... | collective-permute-start | bytes 147464
  1154.2 65.7 %collective-permute-start.34 = (f32[8,1536]{1,0:T(8,128)S(1)}, f32[8,1536]{1,0:T(8,128)S(1)}, u32[]{:S(2)}, u32[]{:S(2)}) collective-permute-start(f32[8,1536]{1,0:T(8,128)S(1)} %fusion), channel_id=1, source_target_pairs={{0,31},{1,32},{2,33},{3,34},{4,35},{5,36},{6,37},{7,38},{8,39},{9,... | collective-permute-start | bytes 147464
  1167.4 65.7 %collective-permute-start.33 = (f32[8,1536]{1,0:T(8,128)S(1)}, f32[8,1536]{1,0:T(8,128)S(1)}, u32[]{:S(2)}, u32[]{:S(2)}) collective-permute-start(f32[8,1536]{1,0:T(8,128)S(1)} %fusion), channel_id=1, source_target_pairs={{0,30},{1,31},{2,32},{3,33},{4,34},{5,35},{6,36},{7,37},{8,38},{9,... | collective-permute-start | bytes 147464
  1180.5 65.7 %collective-permute-start.32 = (f32[8,1536]{1,0:T(8,128)S(1)}, f32[8,1536]{1,0:T(8,128)S(1)}, u32[]{:S(2)}, u32[]{:S(2)}) collective-permute-start(f32[8,1536]{1,0:T(8,128)S(1)} %fusion), channel_id=1, source_target_pairs={{0,29},{1,30},{2,31},{3,32},{4,33},{5,34},{6,35},{7,36},{8,37},{9,... | collective-permute-start | bytes 147464
  1193.7 65.7 %collective-permute-start.31 = (f32[8,1536]{1,0:T(8,128)S(1)}, f32[8,1536]{1,0:T(8,128)S(1)}, u32[]{:S(2)}, u32[]{:S(2)}) collective-permute-start(f32[8,1536]{1,0:T(8,128)S(1)} %fusion), channel_id=1, source_target_pairs={{0,28},{1,29},{2,30},{3,31},{4,32},{5,33},{6,34},{7,35},{8,36},{9,... | collective-permute-start | bytes 147464
  1206.8 65.7 %collective-permute-start.30 = (f32[8,1536]{1,0:T(8,128)S(1)}, f32[8,1536]{1,0:T(8,128)S(1)}, u32[]{:S(2)}, u32[]{:S(2)}) collective-permute-start(f32[8,1536]{1,0:T(8,128)S(1)} %fusion), channel_id=1, source_target_pairs={{0,27},{1,28},{2,29},{3,30},{4,31},{5,32},{6,33},{7,34},{8,35},{9,... | collective-permute-start | bytes 147464
  1220.0 65.7 %collective-permute-start.29 = (f32[8,1536]{1,0:T(8,128)S(1)}, f32[8,1536]{1,0:T(8,128)S(1)}, u32[]{:S(2)}, u32[]{:S(2)}) collective-permute-start(f32[8,1536]{1,0:T(8,128)S(1)} %fusion), channel_id=1, source_target_pairs={{0,26},{1,27},{2,28},{3,29},{4,30},{5,31},{6,32},{7,33},{8,34},{9,... | collective-permute-start | bytes 147464
  1233.1 65.7 %collective-permute-start.28 = (f32[8,1536]{1,0:T(8,128)S(1)}, f32[8,1536]{1,0:T(8,128)S(1)}, u32[]{:S(2)}, u32[]{:S(2)}) collective-permute-start(f32[8,1536]{1,0:T(8,128)S(1)} %fusion), channel_id=1, source_target_pairs={{0,25},{1,26},{2,27},{3,28},{4,29},{5,30},{6,31},{7,32},{8,33},{9,... | collective-permute-start | bytes 147464
  1246.3 65.7 %collective-permute-start.27 = (f32[8,1536]{1,0:T(8,128)S(1)}, f32[8,1536]{1,0:T(8,128)S(1)}, u32[]{:S(2)}, u32[]{:S(2)}) collective-permute-start(f32[8,1536]{1,0:T(8,128)S(1)} %fusion), channel_id=1, source_target_pairs={{0,24},{1,25},{2,26},{3,27},{4,28},{5,29},{6,30},{7,31},{8,32},{9,... | collective-permute-start | bytes 147464
  1259.4 65.7 %collective-permute-start.26 = (f32[8,1536]{1,0:T(8,128)S(1)}, f32[8,1536]{1,0:T(8,128)S(1)}, u32[]{:S(2)}, u32[]{:S(2)}) collective-permute-start(f32[8,1536]{1,0:T(8,128)S(1)} %fusion), channel_id=1, source_target_pairs={{0,23},{1,24},{2,25},{3,26},{4,27},{5,28},{6,29},{7,30},{8,31},{9,... | collective-permute-start | bytes 147464
  1272.6 65.7 %collective-permute-start.25 = (f32[8,1536]{1,0:T(8,128)S(1)}, f32[8,1536]{1,0:T(8,128)S(1)}, u32[]{:S(2)}, u32[]{:S(2)}) collective-permute-start(f32[8,1536]{1,0:T(8,128)S(1)} %fusion), channel_id=1, source_target_pairs={{0,22},{1,23},{2,24},{3,25},{4,26},{5,27},{6,28},{7,29},{8,30},{9,... | collective-permute-start | bytes 147464
  1285.7 65.7 %collective-permute-start.24 = (f32[8,1536]{1,0:T(8,128)S(1)}, f32[8,1536]{1,0:T(8,128)S(1)}, u32[]{:S(2)}, u32[]{:S(2)}) collective-permute-start(f32[8,1536]{1,0:T(8,128)S(1)} %fusion), channel_id=1, source_target_pairs={{0,21},{1,22},{2,23},{3,24},{4,25},{5,26},{6,27},{7,28},{8,29},{9,... | collective-permute-start | bytes 147464
  1298.9 65.7 %collective-permute-start.23 = (f32[8,1536]{1,0:T(8,128)S(1)}, f32[8,1536]{1,0:T(8,128)S(1)}, u32[]{:S(2)}, u32[]{:S(2)}) collective-permute-start(f32[8,1536]{1,0:T(8,128)S(1)} %fusion), channel_id=1, source_target_pairs={{0,20},{1,21},{2,22},{3,23},{4,24},{5,25},{6,26},{7,27},{8,28},{9,... | collective-permute-start | bytes 147464
  1312.0 65.7 %collective-permute-start.22 = (f32[8,1536]{1,0:T(8,128)S(1)}, f32[8,1536]{1,0:T(8,128)S(1)}, u32[]{:S(2)}, u32[]{:S(2)}) collective-permute-start(f32[8,1536]{1,0:T(8,128)S(1)} %fusion), channel_id=1, source_target_pairs={{0,19},{1,20},{2,21},{3,22},{4,23},{5,24},{6,25},{7,26},{8,27},{9,... | collective-permute-start | bytes 147464
  1325.2 65.7 %collective-permute-start.21 = (f32[8,1536]{1,0:T(8,128)S(1)}, f32[8,1536]{1,0:T(8,128)S(1)}, u32[]{:S(2)}, u32[]{:S(2)}) collective-permute-start(f32[8,1536]{1,0:T(8,128)S(1)} %fusion), channel_id=1, source_target_pairs={{0,18},{1,19},{2,20},{3,21},{4,22},{5,23},{6,24},{7,25},{8,26},{9,... | collective-permute-start | bytes 147464
  1443.5 65.7 %collective-permute-start.12 = (f32[8,1536]{1,0:T(8,128)S(1)}, f32[8,1536]{1,0:T(8,128)S(1)}, u32[]{:S(2)}, u32[]{:S(2)}) collective-permute-start(f32[8,1536]{1,0:T(8,128)S(1)} %fusion), channel_id=1, source_target_pairs={{0,9},{1,10},{2,11},{3,12},{4,13},{5,14},{6,15},{7,16},{8,17},{9,1... | collective-permute-start | bytes 147464
  1456.7 65.7 %collective-permute-start.11 = (f32[8,1536]{1,0:T(8,128)S(1)}, f32[8,1536]{1,0:T(8,128)S(1)}, u32[]{:S(2)}, u32[]{:S(2)}) collective-permute-start(f32[8,1536]{1,0:T(8,128)S(1)} %fusion), channel_id=1, source_target_pairs={{0,8},{1,9},{2,10},{3,11},{4,12},{5,13},{6,14},{7,15},{8,16},{9,17... | collective-permute-start | bytes 147464
  1469.8 65.7 %collective-permute-start.10 = (f32[8,1536]{1,0:T(8,128)S(1)}, f32[8,1536]{1,0:T(8,128)S(1)}, u32[]{:S(2)}, u32[]{:S(2)}) collective-permute-start(f32[8,1536]{1,0:T(8,128)S(1)} %fusion), channel_id=1, source_target_pairs={{0,7},{1,8},{2,9},{3,10},{4,11},{5,12},{6,13},{7,14},{8,15},{9,16}... | collective-permute-start | bytes 147464
  1483.0 65.7 %collective-permute-start.9 = (f32[8,1536]{1,0:T(8,128)S(1)}, f32[8,1536]{1,0:T(8,128)S(1)}, u32[]{:S(2)}, u32[]{:S(2)}) collective-permute-start(f32[8,1536]{1,0:T(8,128)S(1)} %fusion), channel_id=1, source_target_pairs={{0,6},{1,7},{2,8},{3,9},{4,10},{5,11},{6,12},{7,13},{8,14},{9,15},... | collective-permute-start | bytes 147464
  1496.1 66.3 %collective-permute-start.8 = (f32[8,1536]{1,0:T(8,128)S(1)}, f32[8,1536]{1,0:T(8,128)}, u32[]{:S(2)}, u32[]{:S(2)}) collective-permute-start(f32[8,1536]{1,0:T(8,128)S(1)} %fusion), channel_id=1, source_target_pairs={{0,5},{1,6},{2,7},{3,8},{4,9},{5,10},{6,11},{7,12},{8,13},{9,14},{... | collective-permute-start | bytes 147464
  (109 other events, 10708.4 us)
Sparse Core Ops, SparseCore 0:
  9.9 732.2 all-gather.2
  2022.9 304.7 all-reduce.5
